TPU v7x, 256 devices: a whole 4x4x8 slice. The times are simulated.
256 devices in a mesh: pipe: 8 (over x_lo, y), dp: 32 (over x_hi, z, core).
Axes of the slice: x: 4 (x_hi: 2, x_lo: 2; x = x_hi * 2 + x_lo), y: 4, z: 8, core: 2. Of those that a mesh axis runs over, the one named last changes fastest.
Arguments:
- x_down: bfloat16 [4096, 4096], P('dp'), may hold values from -6 to 6
- x_up: bfloat16 [4096, 4096], P('dp'), may hold values from -6 to 6
- cot_down: bfloat16 [4096, 4096], P('dp'), may hold values from -6 to 6
- cot_up: bfloat16 [4096, 4096], P('dp'), may hold values from -6 to 6
- w_qkv: bfloat16 [8, 4096, 384], P('pipe', 'dp'), may hold values from -0.09375 to 0.09375
- w_out: bfloat16 [8, 128, 4096], P('pipe', None, 'dp'), may hold values from -0.5 to 0.5
- block_mask: int32 [4, 4], replicated, may hold values from 0 to 1, as said below
Outputs:
- grad_qkv: float32 [8, 4096, 384], P('pipe', 'dp')
- grad_out: float32 [8, 128, 4096], P('pipe', None, 'dp')
Inputs may be any that keep to these rules, and one draw needn't show every extreme that they name: block_mask is 1 on the diagonal and 0 above it.
All inputs are finite; a program needn't handle non-finite values.
Results may differ from a plain program's by a relative error of at most 0.04.
Values may be sent and summed in bfloat16 or wider, within the bound.
A program may use at most 128 MiB of HBM per device.

v0:
```python
import functools

import jax
import jax.numpy as jnp
from jax import lax
from jax.experimental import pallas as pl
from jax.experimental.pallas import tpu as pltpu
from jax.sharding import PartitionSpec as P

BLK = 32
HEAD = 128
XH = 2
CORES = 2
BF = jnp.bfloat16
F32 = jnp.float32

NT = (((1,), (1,)), ((), ()))
TN = (((0,), (0,)), ((), ()))


def mm(a, b):
    return jnp.dot(a, b, preferred_element_type=F32)


def mm_nt(a, b):
    return lax.dot_general(a, b, NT, preferred_element_type=F32)


def mm_tn(a, b):
    return lax.dot_general(a, b, TN, preferred_element_type=F32)


def kernel(
    n_pipe,
    n_dp,
    x_down, x_up, cot_down, cot_up, wq_ref, wo_ref, mask_ref,
    gq_ref, go_ref,
    allowed, wpack, w1b, w, x, dy, agb, p1, soft, att, t1, rbuf, e_buf,
    rs_send, rs_recv, gh_send, gh_recv, ghb, ds_send, ds_recv, da, da0,
    g, gd, gxr, gz, gx, hp, out,
    load_sem, w1_send, w1_recv, w2_send, w2_recv, wz_send, wz_recv, wc_send, wc_recv,
    rs_ssem, rs_rsem, ag_ssem, ag_rsem, gh_ssem, gh_rsem, ha_ssem, ha_rsem, ds_ssem, ds_rsem, da_ssem, da_rsem,
    gc_send, gc_recv, gs_send, gs_recv, gz_send, gz_recv, hp_send, hp_recv, gf_send, gf_recv,
):
    pairs = n_pipe // 2
    n_z = n_dp // (XH * CORES)
    n_i = n_dp // n_pipe
    rows = x.shape[2]
    feat = x.shape[3]
    dim = feat * n_pipe
    group = w.shape[3]
    per_block = n_pipe // XH
    rb = rows // n_pipe
    end = pairs - 1
    q3 = 3 * HEAD
    width = 4 * HEAD
    scale = HEAD ** (-0.5)

    me = lax.axis_index("pipe")
    d = lax.axis_index("dp")
    xh = d // (n_z * CORES)
    z = (d // CORES) % n_z
    c = d % CORES

    def dp_at(xh_, z_, c_):
        return xh_ * (n_z * CORES) + z_ * CORES + c_

    def peer(k):
        return lax.rem(me + 1 + k, n_pipe)

    def z_peer(k):
        return dp_at(xh, lax.rem(z + 1 + k, n_z), c)

    sibling = dp_at(xh, z, 1 - c)
    xh_peer = dp_at(1 - xh, z, c)
    piece = group // XH
    my_rows = pl.ds(pl.multiple_of(xh * piece, piece), piece)
    other_rows = pl.ds(pl.multiple_of((1 - xh) * piece, piece), piece)

    def spread_to(s):
        u = (d % n_i) * per_block + s
        return u // CORES, u % CORES

    to_pipe = d // n_i
    my_u = z * CORES + c
    my_s = my_u % per_block

    def remote(src, dst, ssem, rsem, pp, dd):
        return pltpu.make_async_remote_copy(
            src_ref=src, dst_ref=dst, send_sem=ssem, recv_sem=rsem,
            device_id={"pipe": pp, "dp": dd}, device_id_type=pl.DeviceIdType.MESH,
        )

    def wait_bytes(ref, sem):
        pltpu.make_async_copy(ref, ref, sem).wait()

    def layers_of(pair):
        return pl.ds(2 * pair, 2)

    barrier = pltpu.get_barrier_semaphore()

    def greet(pp, dd):
        pl.semaphore_signal(
            barrier, inc=1, device_id={"pipe": pp, "dp": dd},
            device_id_type=pl.DeviceIdType.MESH,
        )

    for s in range(per_block):
        uz, uc = spread_to(s)
        for h in range(XH):
            dd = dp_at(h, uz, uc)

            @pl.when(dd != d)
            def _():
                greet(me, dd)

    for j in range(n_pipe):

        @pl.when(n_i * j + my_u // per_block != d)
        def _():
            greet(me, n_i * j + my_u // per_block)

    for k in range(n_z - 1):
        greet(me, z_peer(k))
    greet(me, sibling)
    greet(me, xh_peer)
    for k in range(n_pipe - 1):
        greet(peer(k), d)
        greet(peer(k), xh_peer)

    cols = pl.ds(pl.multiple_of(me * feat, feat), feat)
    top = 2 * pairs - 1
    loads = [
        pltpu.make_async_copy(x_down.at[:, cols], x.at[0, 0], load_sem.at[0]),
        pltpu.make_async_copy(x_up.at[:, cols], x.at[0, 1], load_sem.at[1]),
        pltpu.make_async_copy(cot_down.at[:, cols], dy.at[top, 0], load_sem.at[2]),
        pltpu.make_async_copy(cot_up.at[:, cols], dy.at[top, 1], load_sem.at[3]),
    ]
    for copy in loads:
        copy.start()

    blocks = mask_ref.shape[0]
    row = lax.broadcasted_iota(jnp.int32, (rows, rows), 0)
    col = lax.broadcasted_iota(jnp.int32, (rows, rows), 1)
    read = jnp.zeros((rows, rows), jnp.int32)
    for i in range(blocks):
        for j in range(blocks):
            inside = (row // (rows // blocks) == i) & (col // (rows // blocks) == j)
            read = jnp.where(inside, mask_ref[i, j], read)
    allowed[...] = jnp.where((read == 1) & (col <= row), 1.0, 0.0)

    wpack[:, :q3] = wq_ref[0]
    wpack[:, q3:] = wo_ref[0].astype(F32).T.astype(BF)

    itself = jnp.where(my_u // per_block == d % n_i, 1, 0)
    pl.semaphore_wait(barrier, 4 * n_pipe + n_z - 1 - 2 * itself)

    for s in range(per_block):
        uz, uc = spread_to(s)
        for h in range(XH):
            dd = dp_at(h, uz, uc)
            src = wpack.at[pl.ds((XH * s + h) * piece, piece)]

            @pl.when(dd != d)
            def _():
                remote(src, w1b.at[to_pipe], w1_send.at[XH * s + h], w1_recv.at[0], me, dd).start()

            @pl.when(dd == d)
            def _():
                pltpu.make_async_copy(src, w1b.at[to_pipe], w1_recv.at[0]).start()

    wait_bytes(w1b, w1_recv.at[0])
    held = w.at[me, z, c, my_rows]
    for k in range(n_pipe - 1):
        to = peer(k)
        remote(w1b.at[to], held, w2_send.at[0], w2_recv.at[0], to, d).start()
        remote(w1b.at[to], held, w2_send.at[1], w2_recv.at[0], to, xh_peer).start()
    remote(w1b.at[me], held, w2_send.at[1], w2_recv.at[0], me, xh_peer).start()
    pltpu.make_async_copy(w1b.at[me], held, w2_recv.at[0]).start()
    wait_bytes(w.at[:, z, c], w2_recv.at[0])

    def start_wz(layer):
        mine = w.at[layer, z, c]
        for k in range(n_z - 1):
            remote(mine, mine, wz_send.at[layer], wz_recv.at[layer], me, z_peer(k)).start()

    def start_wc(layer):
        wait_bytes(w.at[layer, pl.ds(0, n_z - 1), c], wz_recv.at[layer])
        mine = w.at[layer, :, c]
        remote(mine, mine, wc_send.at[layer], wc_recv.at[layer], me, sibling).start()

    def wait_wc(layer):
        wait_bytes(w.at[layer, :, 1 - c], wc_recv.at[layer])

    start_wz(0)
    start_wz(1)

    def weight(layer):
        return w[layer].reshape(feat, width)

    for copy in loads:
        copy.wait()

    own = pl.ds(pl.multiple_of(me * rb, rb), rb)

    def scatter(src, dst, ssem, rsem):
        for k in range(n_pipe - 1):
            to = peer(k)
            remote(
                src.at[pl.ds(pl.multiple_of(to * rb, rb), rb)], dst.at[n_pipe - 2 - k], ssem, rsem, to, d
            ).start()

    def gather(ref, ssem, rsem):
        for k in range(n_pipe - 1):
            remote(ref.at[own], ref.at[own], ssem, rsem, peer(k), d).start()

    def wait_gather(ref, ssem, rsem):
        part = ref.at[pl.ds(0, rows - rb)]
        wait_bytes(part, rsem)
        wait_bytes(part, ssem)

    def start_rs_first(cas, xl, pair):
        xf = xl.astype(F32)
        sq = jnp.sum(xf * xf, axis=-1, keepdims=True)
        first = mm(xl, weight(2 * pair))
        rs_send[cas, 0, :, :q3] = first[:, :q3].astype(BF)
        rs_send[cas, 0, :, q3:] = jnp.broadcast_to(sq, (rows, HEAD)).astype(BF)
        scatter(rs_send.at[cas, 0], rs_recv.at[cas, 0], rs_ssem.at[cas, 0], rs_rsem.at[cas, 0])
        rs_send[cas, 1, :, :HEAD] = first[:, q3:].astype(BF)

    def start_rs_second(cas, xl, pair):
        rs_send[cas, 1, :, HEAD:] = mm(xl, weight(2 * pair + 1)[:, :q3]).astype(BF)
        scatter(rs_send.at[cas, 1], rs_recv.at[cas, 1], rs_ssem.at[cas, 1], rs_rsem.at[cas, 1])

    def start_ag(pair, cas, half):
        wait_bytes(rs_recv.at[cas, half], rs_rsem.at[cas, half])
        wait_bytes(rs_recv.at[cas, half], rs_ssem.at[cas, half])
        total = rs_send[cas, half, own].astype(F32)
        for k in range(n_pipe - 1):
            total = total + rs_recv[cas, half, k].astype(F32)
        if half == 0:
            norm = total[:, q3:]
            r = lax.rsqrt(norm * (1.0 / dim) + 1e-6)
            high = norm.astype(BF).astype(F32)
            lane = lax.broadcasted_iota(jnp.int32, norm.shape, 1)
            agb[pair, cas, 0, own, :q3] = (total[:, :q3] * r[:, :1]).astype(BF)
            agb[pair, cas, 0, own, q3:] = jnp.where(lane < HEAD // 2, high, norm - high).astype(BF)
        else:
            agb[pair, cas, 1, own] = total.astype(BF)
        gather(agb.at[pair, cas, half], ag_ssem.at[cas, half], ag_rsem.at[cas, half])

    def start_rs_gh(pair):
        w0 = weight(2 * pair)[:, q3:]
        gh_send[:, :q3] = mm_tn(w0, weight(2 * pair + 1)[:, :q3]).astype(BF)
        gh_send[:, q3:] = mm_tn(w0, w0).astype(BF)
        for k in range(n_pipe - 1):
            to = peer(k)
            gr = HEAD // n_pipe
            remote(
                gh_send.at[pl.ds(pl.multiple_of(to * gr, gr), gr)], gh_recv.at[pair, n_pipe - 2 - k],
                gh_ssem.at[0], gh_rsem.at[pair], to, d,
            ).start()

    gh_own = pl.ds(pl.multiple_of(me * (HEAD // n_pipe), HEAD // n_pipe), HEAD // n_pipe)

    def start_ag_gh(pair):
        wait_bytes(gh_recv.at[pair], gh_rsem.at[pair])
        wait_bytes(gh_recv.at[pair], gh_ssem.at[0])
        total = gh_send[gh_own].astype(F32)
        for k in range(n_pipe - 1):
            total = total + gh_recv[pair, k].astype(F32)
        ghb[pair, gh_own] = total.astype(BF)
        ref = ghb.at[pair, gh_own]
        for k in range(n_pipe - 1):
            remote(ref, ref, ha_ssem.at[pair], ha_rsem.at[pair], peer(k), d).start()

    def wait_ag_gh(pair):
        part = ghb.at[pair, pl.ds(0, HEAD - HEAD // n_pipe)]
        wait_bytes(part, ha_rsem.at[pair])
        wait_bytes(part, ha_ssem.at[pair])

    def attend(layer, cas, pr):
        s = mm_nt(pr[:, :HEAD], pr[:, HEAD : 2 * HEAD]) * scale
        s = jnp.where(allowed[...] > 0.5, s, -1e30)
        ex = jnp.exp(s - jnp.max(s, axis=-1, keepdims=True))
        sm = (ex / jnp.sum(ex, axis=-1, keepdims=True)).astype(BF)
        soft[layer, cas] = sm
        a = mm(sm, pr[:, 2 * HEAD : q3]).astype(BF)
        att[layer, cas] = a
        return a

    start_wc(0)
    wait_wc(0)
    for cas in range(2):
        start_rs_first(cas, x[0, cas], 0)
    start_wc(1)
    if pairs > 1:
        start_wz(2)
        start_wz(3)
    wait_wc(1)
    for cas in range(2):
        start_rs_second(cas, x[0, cas], 0)
    start_rs_gh(0)

    def start_ds(cas, dyl, pair):
        ds_send[cas, :, :HEAD] = mm(dyl, weight(2 * pair)[:, q3:]).astype(BF)
        ds_send[cas, :, HEAD:] = mm(dyl, weight(2 * pair + 1)[:, q3:]).astype(BF)
        scatter(ds_send.at[cas], ds_recv.at[cas], ds_ssem.at[cas], ds_rsem.at[cas])

    def start_da(cas):
        wait_bytes(ds_recv.at[cas], ds_rsem.at[cas])
        wait_bytes(ds_recv.at[cas], ds_ssem.at[cas])
        total = ds_send[cas, own].astype(F32)
        for k in range(n_pipe - 1):
            total = total + ds_recv[cas, k].astype(F32)
        da[cas, own] = total.astype(BF)
        gather(da.at[cas], da_ssem.at[cas], da_rsem.at[cas])

    def forward(pair, carry):
        l0 = 2 * pair
        l1 = l0 + 1
        for cas in range(2):
            for half in range(2):
                start_ag(pair, cas, half)

        @pl.when(pair == 0)
        def _():
            start_ag_gh(0)

        @pl.when(pair == end)
        def _():
            for cas in range(2):
                start_ds(cas, dy[top, cas], end)

        @pl.when(pair < end)
        def _():
            start_wc(l0 + 2)
            start_wc(l1 + 2)

            @pl.when(pair + 2 < pairs)
            def _():
                start_wz(l0 + 4)
                start_wz(l1 + 4)

            wait_wc(l0 + 2)
            wait_wc(l1 + 2)
            start_rs_gh(pair + 1)

        for cas in range(2):
            wait_gather(agb.at[pair, cas, 0], ag_ssem.at[cas, 0], ag_rsem.at[cas, 0])
            a0 = attend(l0, cas, agb[pair, cas, 0, :, :q3])
            half_lane = width - HEAD // 2
            n0 = (
                agb[pair, cas, 0, :, q3 : q3 + 1].astype(F32)
                + agb[pair, cas, 0, :, half_lane : half_lane + 1].astype(F32)
            )
            x1 = (x[l0, cas].astype(F32) + mm_nt(a0, weight(l0)[:, q3:])).astype(BF)
            x[l1, cas] = x1
            if cas == 0:
                wait_ag_gh(pair)
            agh = mm(a0, ghb[pair])
            wait_gather(agb.at[pair, cas, 1], ag_ssem.at[cas, 1], ag_rsem.at[cas, 1])
            c0 = agb[pair, cas, 1, :, :HEAD].astype(F32)
            v = agh[:, q3:]
            n1 = n0 + jnp.sum(a0.astype(F32) * (2.0 * c0 + v), axis=-1, keepdims=True)
            t1[pair, cas] = c0 + v
            r0 = lax.rsqrt(n0 * (1.0 / dim) + 1e-6)
            r1 = lax.rsqrt(jnp.maximum(n1, 0.0) * (1.0 / dim) + 1e-6)
            rbuf[l0, cas] = jnp.broadcast_to(r0, (rows, HEAD))
            rbuf[l1, cas] = jnp.broadcast_to(r1, (rows, HEAD))
            pr1 = ((agb[pair, cas, 1, :, HEAD:].astype(F32) + agh[:, :q3]) * r1).astype(BF)
            p1[pair, cas] = pr1
            a1 = attend(l1, cas, pr1)

            @pl.when(pair < end)
            def _():
                x2 = (x1.astype(F32) + mm_nt(a1, weight(l1)[:, q3:])).astype(BF)
                x[l1 + 1, cas] = x2
                start_rs_first(cas, x2, pair + 1)
                start_rs_second(cas, x2, pair + 1)

        @pl.when(pair < end)
        def _():
            start_ag_gh(pair + 1)

        return carry

    lax.fori_loop(0, pairs, forward, 0)

    def attend_back(layer, cas, slot, pr, da):
        sm = soft[layer, cas]
        smf = sm.astype(F32)
        r = rbuf[layer, cas]
        dv = mm_tn(sm, da)
        dsm = mm_nt(da, pr[:, 2 * HEAD :])
        ds = (smf * (dsm - jnp.sum(dsm * smf, axis=-1, keepdims=True)) * scale).astype(BF)
        dq = mm(ds, pr[:, HEAD : 2 * HEAD])
        dk = mm_tn(ds, pr[:, :HEAD])
        prf = pr.astype(F32)
        dot = jnp.sum(
            dq * prf[:, :HEAD] + dk * prf[:, HEAD : 2 * HEAD] + dv * prf[:, 2 * HEAD :], axis=-1, keepdims=True
        )
        e_buf[slot, cas, :, :HEAD] = (dq * r).astype(BF)
        e_buf[slot, cas, :, HEAD : 2 * HEAD] = (dk * r).astype(BF)
        e_buf[slot, cas, :, 2 * HEAD :] = (dv * r).astype(BF)
        return r[:, :1] * r[:, :1] * dot * (1.0 / dim)

    def weight_grads(layer, i):
        xl = x[layer].reshape(2 * rows, feat)
        dyl = dy[layer].reshape(2 * rows, feat)
        gq = mm_tn(xl, e_buf[i].reshape(2 * rows, q3)).astype(BF)
        go = mm_tn(dyl, att[layer].reshape(2 * rows, HEAD)).astype(BF)
        g[layer, :, :, :, :q3] = gq.reshape(n_z, CORES, group, q3)
        g[layer, :, :, :, q3:] = go.reshape(n_z, CORES, group, HEAD)
        remote(
            g.at[layer, :, 1 - c], gd.at[layer], gc_send.at[layer], gc_recv.at[layer], me, sibling
        ).start()

    def backward(t, carry):
        pair = end - t
        l0 = 2 * pair
        l1 = l0 + 1

        @pl.when(t < pairs)
        def _():
            for cas in range(2):
                start_da(cas)

        @pl.when((t >= 1) & (t < pairs + 1))
        def _():
            for i in (1, 0):
                lay = 2 * (pair + 1) + i
                wait_bytes(gd.at[lay], gc_recv.at[lay])
                mine = (lay, slice(None), pl.ds(c, 1))
                g[mine] = (g[mine].astype(F32) + gd[lay][:, None].astype(F32)).astype(BF)
                remote(
                    g.at[lay, :, c, other_rows], gxr.at[lay], gs_send.at[lay], gs_recv.at[lay], me, xh_peer
                ).start()

        @pl.when(t < pairs)
        def _():
            for cas in range(2):
                wait_gather(da.at[cas], da_ssem.at[cas], da_rsem.at[cas])
                cc1 = attend_back(l1, cas, 1, p1[pair, cas], da[cas, :, HEAD:])
                e1 = e_buf[1, cas]
                da0[cas] = (da[cas, :, :HEAD].astype(F32) + mm_nt(e1, ghb[pair][:, :q3]) - cc1 * t1[pair, cas]).astype(BF)
                dy[l0, cas] = (
                    dy[l1, cas].astype(F32) + mm_nt(e1, weight(l1)[:, :q3]) - x[l1, cas].astype(F32) * cc1
                ).astype(BF)

                @pl.when(pair > 0)
                def _():
                    cc0 = attend_back(l0, cas, 0, agb[pair, cas, 0, :, :q3], da0[cas])
                    dy_new = (
                        dy[l0, cas].astype(F32)
                        + mm_nt(e_buf[0, cas], weight(l0)[:, :q3])
                        - x[l0, cas].astype(F32) * cc0
                    ).astype(BF)
                    dy[l0 - 1, cas] = dy_new
                    start_ds(cas, dy_new, pair - 1)

            @pl.when(pair == 0)
            def _():
                weight_grads(l1, 1)
                for cas in range(2):
                    attend_back(l0, cas, 0, agb[pair, cas, 0, :, :q3], da0[cas])

        @pl.when((t >= 1) & (t < pairs + 1))
        def _():
            for i in (1, 0):
                lay = 2 * (pair + 1) + i
                wait_bytes(gxr.at[lay], gs_recv.at[lay])
                mine = (lay, slice(None), pl.ds(c, 1), my_rows)
                g[mine] = (g[mine].astype(F32) + gxr[lay][:, None].astype(F32)).astype(BF)
                for k in range(n_z - 1):
                    to_z = lax.rem(z + 1 + k, n_z)
                    remote(
                        g.at[lay, to_z, c, my_rows], gz.at[lay, n_z - 2 - k],
                        gz_send.at[lay], gz_recv.at[lay], me, z_peer(k),
                    ).start()

        @pl.when((t >= 2) & (t < pairs + 2))
        def _():
            for i in (1, 0):
                lay = 2 * (pair + 2) + i
                wait_bytes(gz.at[lay], gz_recv.at[lay])
                total = g[lay, z, c, my_rows].astype(F32)
                for k in range(n_z - 1):
                    total = total + gz[lay, k].astype(F32)
                gx[lay] = total.astype(BF)

        @pl.when((t < pairs) & (pair > 0))
        def _():
            weight_grads(l1, 1)

        @pl.when(t < pairs)
        def _():
            weight_grads(l0, 0)

        return carry

    lax.fori_loop(0, pairs + 2, backward, 0)

    for k in range(n_pipe - 1):
        to = peer(k)
        remote(gx.at[to], hp.at[me], hp_send.at[0], hp_recv.at[0], to, d).start()
    hp[pl.ds(me, 1)] = gx[pl.ds(me, 1)]
    wait_bytes(hp.at[pl.ds(0, n_pipe - 1)], hp_recv.at[0])
    for k in range(n_pipe):
        pp = lax.rem(me + k, n_pipe)
        dd = n_i * pp + my_u // per_block

        @pl.when(dd != d)
        def _():
            remote(hp.at[pp], out.at[my_s, xh], gf_send.at[pp], gf_recv.at[0], me, dd).start()

        @pl.when(dd == d)
        def _():
            pltpu.make_async_copy(hp.at[pp], out.at[my_s, xh], gf_recv.at[0]).start()

    wait_bytes(out, gf_recv.at[0])
    full = out[...].astype(F32).reshape(per_block * group, width)
    gq_ref[0] = full[:, :q3]
    go_ref[0] = full[:, q3:].T

    for s in range(per_block):
        uz, uc = spread_to(s)
        for h in range(XH):
            dd = dp_at(h, uz, uc)

            @pl.when(dd != d)
            def _():
                wait_bytes(wpack.at[pl.ds((XH * s + h) * piece, piece)], w1_send.at[XH * s + h])

    wait_bytes(w1b.at[pl.ds(0, n_pipe - 1)], w2_send.at[0])
    wait_bytes(w1b, w2_send.at[1])
    wait_bytes(hp.at[pl.ds(0, n_pipe - 1)], hp_send.at[0])

    def drain(lay, carry):
        wait_bytes(w.at[lay, pl.ds(0, n_z - 1), c], wz_send.at[lay])
        wait_bytes(w.at[lay, :, c], wc_send.at[lay])
        wait_bytes(gd.at[lay], gc_send.at[lay])
        wait_bytes(gxr.at[lay], gs_send.at[lay])
        wait_bytes(gz.at[lay], gz_send.at[lay])

        @pl.when(n_i * lay + my_u // per_block != d)
        def _():
            wait_bytes(hp.at[lay], gf_send.at[lay])

        return carry

    lax.fori_loop(0, n_pipe, drain, 0)


def per_device(x_down, x_up, cot_down, cot_up, w_qkv, w_out, block_mask):
    n_pipe, n_dp = lax.axis_size("pipe"), lax.axis_size("dp")
    rows, dim = x_down.shape
    feat = dim // n_pipe
    n_z = n_dp // (XH * CORES)
    group = feat // (n_z * CORES)
    per_block = n_pipe // XH
    width = 4 * HEAD
    rb = rows // n_pipe
    layers = n_pipe
    pairs = layers // 2
    any_spec = pl.BlockSpec(memory_space=pl.ANY)
    vmem = pl.BlockSpec(memory_space=pltpu.VMEM)
    dma = pltpu.SemaphoreType.DMA
    return pl.pallas_call(
        functools.partial(kernel, n_pipe, n_dp),
        out_shape=(
            jax.ShapeDtypeStruct(w_qkv.shape, F32),
            jax.ShapeDtypeStruct(w_out.shape, F32),
        ),
        in_specs=[any_spec] * 4 + [vmem] * 2 + [pl.BlockSpec(memory_space=pltpu.SMEM)],
        out_specs=(vmem, vmem),
        scratch_shapes=[
            pltpu.VMEM((rows, rows), F32),
            pltpu.VMEM((per_block * group, width), BF),
            pltpu.VMEM((n_pipe, group // XH, width), BF),
            pltpu.VMEM((layers, n_z, CORES, group, width), BF),
            pltpu.VMEM((layers, 2, rows, feat), BF),
            pltpu.VMEM((layers, 2, rows, feat), BF),
            pltpu.VMEM((pairs, 2, 2, rows, width), BF),
            pltpu.VMEM((pairs, 2, rows, 3 * HEAD), BF),
            pltpu.VMEM((layers, 2, rows, rows), BF),
            pltpu.VMEM((layers, 2, rows, HEAD), BF),
            pltpu.VMEM((pairs, 2, rows, HEAD), F32),
            pltpu.VMEM((layers, 2, rows, HEAD), F32),
            pltpu.VMEM((2, 2, rows, 3 * HEAD), BF),
            pltpu.VMEM((2, 2, rows, width), BF),
            pltpu.VMEM((2, 2, n_pipe - 1, rb, width), BF),
            pltpu.VMEM((HEAD, width), BF),
            pltpu.VMEM((pairs, n_pipe - 1, HEAD // n_pipe, width), BF),
            pltpu.VMEM((pairs, HEAD, width), BF),
            pltpu.VMEM((2, rows, 2 * HEAD), BF),
            pltpu.VMEM((2, n_pipe - 1, rb, 2 * HEAD), BF),
            pltpu.VMEM((2, rows, 2 * HEAD), BF),
            pltpu.VMEM((2, rows, HEAD), BF),
            pltpu.VMEM((layers, n_z, CORES, group, width), BF),
            pltpu.VMEM((layers, n_z, group, width), BF),
            pltpu.VMEM((layers, n_z, group // XH, width), BF),
            pltpu.VMEM((layers, n_z - 1, group // XH, width), BF),
            pltpu.VMEM((layers, group // XH, width), BF),
            pltpu.VMEM((layers, group // XH, width), BF),
            pltpu.VMEM((per_block, XH, group // XH, width), BF),
            dma((4,)),
            dma((n_pipe,)), dma((1,)),
            dma((2,)), dma((1,)),
            dma((layers,)), dma((layers,)),
            dma((layers,)), dma((layers,)),
            dma((2, 2)), dma((2, 2)), dma((2, 2)), dma((2, 2)),
            dma((1,)), dma((pairs,)), dma((pairs,)), dma((pairs,)),
            dma((2,)), dma((2,)), dma((2,)), dma((2,)),
            dma((layers,)), dma((layers,)),
            dma((layers,)), dma((layers,)),
            dma((layers,)), dma((layers,)),
            dma((1,)), dma((1,)),
            dma((layers,)), dma((1,)),
        ],
        compiler_params=pltpu.CompilerParams(
            collective_id=0, has_side_effects=True, vmem_limit_bytes=60 * 1024 * 1024
        ),
    )(x_down, x_up, cot_down, cot_up, w_qkv, w_out, block_mask)


def solution(mesh):
    placed = (
        P("dp", None),
        P("dp", None),
        P("dp", None),
        P("dp", None),
        P("pipe", "dp", None),
        P("pipe", None, "dp"),
        P(),
    )
    return jax.shard_map(
        per_device,
        mesh=mesh,
        in_specs=placed,
        out_specs=(P("pipe", "dp", None), P("pipe", None, "dp")),
        check_vma=False,
    )
```

profile of v0, /device:TPU:2, one launch (start us, length us, event | category | flops | bytes accessed | tf_op | source)
XLA Modules:
  0.0 170.9 jit_solution(13842061517920814509)
XLA Ops:
  0.6 168.0 %shard_map.86 = (f32[1,128,384]{2,1,0:T(8,128)}, f32[1,128,128]{2,1,0:T(8,128)}) custom-call(bf16[128,4096]{1,0:T(8,128)(2,1)} %x_down.1, bf16[128,4096]{1,0:T(8,128)(2,1)} %x_up.1, bf16[128,4096]{1,0:T(8,128)(2,1)} %cot_down.1, bf16[128,4096]{1,0:T(8,128)(2,1)} %cot_up.1, bf16[1,128,384]{2,1,0:T(8,128)(2,1)} %wq_ref.1, bf16[1,128,128]{2,1,0:T(8,128)(2,1)} %wo_ref.1, ...), custom_call_target="tpu_custom_call" | custom-call | tf_op jit(solution)/shard_map/pallas_call | solution.py:569
  168.6 0.0 copy-start
  168.6 1.6 copy.11
  170.3 0.0 copy-done
  170.3 0.6 copy.12
Async XLA Ops:
  168.6 1.7 copy-start
where the time goes:
time: 173 us; the launch traced here: 171 us
  Pallas kernels  168 us (97%)
  local copies, waits for them, and re-layouts  2.28 us (1%)
    pallas_call x1, Pallas kernels, per_device(): pl.pallas_call(functools.partial(kernel, n_pipe, n_dp), out_shape=(jax.Sh...  168 us

commit v1 on v0

--- a/solution.py
+++ b/solution.py
@@ -179,13 +179,36 @@
     pltpu.make_async_copy(w1b.at[me], held, w2_recv.at[0]).start()
     wait_bytes(w.at[:, z, c], w2_recv.at[0])
 
+    two_steps = n_z == 8
+
+    def z_at(step):
+        return lax.rem(z + step + n_z, n_z)
+
     def start_wz(layer):
         mine = w.at[layer, z, c]
-        for k in range(n_z - 1):
-            remote(mine, mine, wz_send.at[layer], wz_recv.at[layer], me, z_peer(k)).start()
+        steps = ((1, 0), (-1, 0), (2, 2), (-2, 1)) if two_steps else [(k + 1, 0) for k in range(n_z - 1)]
+        for step, sem in steps:
+            remote(
+                mine, mine, wz_send.at[layer], wz_recv.at[layer, sem], me, dp_at(xh, z_at(step), c)
+            ).start()
+
+    def pass_wz(layer):
+        if two_steps:
+            for side, sem in ((1, 1), (-1, 2)):
+                far = w.at[layer, z_at(2 * side), c]
+                half = w.at[layer, z_at(2 * side), c, pl.ds(0 if side == 1 else piece, piece)]
+                wait_bytes(far, wz_recv.at[layer, sem])
+                for ref, step in ((far, -side), (half, -2 * side)):
+                    remote(
+                        ref, ref, wz_send.at[layer], wz_recv.at[layer, 3], me, dp_at(xh, z_at(step), c)
+                    ).start()
 
     def start_wc(layer):
-        wait_bytes(w.at[layer, pl.ds(0, n_z - 1), c], wz_recv.at[layer])
+        if two_steps:
+            wait_bytes(w.at[layer, pl.ds(0, 2), c], wz_recv.at[layer, 0])
+            wait_bytes(w.at[layer, pl.ds(0, 3), c], wz_recv.at[layer, 3])
+        else:
+            wait_bytes(w.at[layer, pl.ds(0, n_z - 1), c], wz_recv.at[layer, 0])
         mine = w.at[layer, :, c]
         remote(mine, mine, wc_send.at[layer], wc_recv.at[layer], me, sibling).start()
 
@@ -289,18 +312,26 @@
         att[layer, cas] = a
         return a
 
+    pass_wz(0)
+    pass_wz(1)
+    if pairs > 1:
+        start_wz(2)
+        start_wz(3)
     start_wc(0)
     wait_wc(0)
     for cas in range(2):
         start_rs_first(cas, x[0, cas], 0)
     start_wc(1)
     if pairs > 1:
-        start_wz(2)
-        start_wz(3)
+        pass_wz(2)
+        pass_wz(3)
     wait_wc(1)
     for cas in range(2):
         start_rs_second(cas, x[0, cas], 0)
     start_rs_gh(0)
+    if pairs > 2:
+        start_wz(4)
+        start_wz(5)
 
     def start_ds(cas, dyl, pair):
         ds_send[cas, :, :HEAD] = mm(dyl, weight(2 * pair)[:, q3:]).astype(BF)
@@ -339,8 +370,13 @@
 
             @pl.when(pair + 2 < pairs)
             def _():
-                start_wz(l0 + 4)
-                start_wz(l1 + 4)
+                pass_wz(l0 + 4)
+                pass_wz(l1 + 4)
+
+            @pl.when(pair + 3 < pairs)
+            def _():
+                start_wz(l0 + 6)
+                start_wz(l1 + 6)
 
             wait_wc(l0 + 2)
             wait_wc(l1 + 2)
@@ -416,6 +452,8 @@
             g.at[layer, :, 1 - c], gd.at[layer], gc_send.at[layer], gc_recv.at[layer], me, sibling
         ).start()
 
+    start_da(0)
+
     def backward(t, carry):
         pair = end - t
         l0 = 2 * pair
@@ -423,8 +461,7 @@
 
         @pl.when(t < pairs)
         def _():
-            for cas in range(2):
-                start_da(cas)
+            start_da(1)
 
         @pl.when((t >= 1) & (t < pairs + 1))
         def _():
@@ -464,6 +501,10 @@
                 weight_grads(l1, 1)
                 for cas in range(2):
                     attend_back(l0, cas, 0, agb[pair, cas, 0, :, :q3], da0[cas])
+
+        @pl.when(t < end)
+        def _():
+            start_da(0)
 
         @pl.when((t >= 1) & (t < pairs + 1))
         def _():
@@ -607,7 +648,7 @@
             dma((4,)),
             dma((n_pipe,)), dma((1,)),
             dma((2,)), dma((1,)),
-            dma((layers,)), dma((layers,)),
+            dma((layers,)), dma((layers, 4)),
             dma((layers,)), dma((layers,)),
             dma((2, 2)), dma((2, 2)), dma((2, 2)), dma((2, 2)),
             dma((1,)), dma((pairs,)), dma((pairs,)), dma((pairs,)),

time: 173 us -> 175 us (1.012)
  no operation moved by 1% of the time
where the time goes in v1:
time: 175 us; the launch traced here: 172 us
  Pallas kernels  169 us (97%)
  local copies, waits for them, and re-layouts  2.28 us (1%)
    pallas_call x1, Pallas kernels, per_device(): pl.pallas_call(functools.partial(kernel, n_pipe, n_dp), out_shape=(jax.Sh...  169 us

profile of v1, /device:TPU:2, one launch (start us, length us, event | category | flops | bytes accessed | tf_op | source)
XLA Modules:
  0.0 171.9 jit_solution(16071653262048010223)
XLA Ops:
  0.6 169.0 %shard_map.86 = (f32[1,128,384]{2,1,0:T(8,128)}, f32[1,128,128]{2,1,0:T(8,128)}) custom-call(bf16[128,4096]{1,0:T(8,128)(2,1)} %x_down.1, bf16[128,4096]{1,0:T(8,128)(2,1)} %x_up.1, bf16[128,4096]{1,0:T(8,128)(2,1)} %cot_down.1, bf16[128,4096]{1,0:T(8,128)(2,1)} %cot_up.1, bf16[1,128,384]{2,1,0:T(8,128)(2,1)} %wq_ref.1, bf16[1,128,128]{2,1,0:T(8,128)(2,1)} %wo_ref.1, ...), custom_call_target="tpu_custom_call" | custom-call | tf_op jit(solution)/shard_map/pallas_call | solution.py:610
  169.6 0.0 copy-start
  169.7 1.6 copy.11
  171.3 0.0 copy-done
  171.3 0.6 copy.12
Async XLA Ops:
  169.6 1.7 copy-start
